TPU v7x, 32 devices: a whole 2x2x4 slice. The times are simulated.
32 devices in a mesh: pipe: 4 (over z), dp: 8 (over y, x, core).
Axes of the slice: x: 2, y: 2, z: 4, core: 2. Of those that a mesh axis runs over, the one named last changes fastest.
Arguments:
- images: bfloat16 [128, 14, 14, 384], P('dp'), may hold values from -6 to 6
- depth_kernel: float32 [7, 7, 384], replicated, may hold values from -0.875 to 0.875
- depth_bias: float32 [384], replicated, may hold values from -3 to 3
- norm_gain: float32 [384], replicated, may hold values from 0.1 to 1.9
- norm_shift: float32 [384], replicated, may hold values from -2 to 2
- up_weight: bfloat16 [384, 1536], replicated, may hold values from -0.3125 to 0.3125
- up_bias: float32 [1536], replicated, may hold values from -2 to 2
- down_weight: bfloat16 [1536, 384], replicated, may hold values from -0.15625 to 0.15625
- down_bias: float32 [384], replicated, may hold values from -2 to 2
- layer_scale: float32 [384], replicated, may hold values from 0.5 to 1.5
- merge_gain: float32 [384], replicated, may hold values from 0.1 to 1.9
- merge_shift: float32 [384], replicated, may hold values from -2 to 2
- patch_weight: bfloat16 [1536, 768], replicated, may hold values from -0.15625 to 0.15625
- patch_bias: float32 [768], replicated, may hold values from -2 to 2
- keep_mask: int32 [128], P('dp'), may hold values 0 or 1
- out_grad: bfloat16 [128, 7, 7, 768], P('dp'), may hold values from -6 to 6
Outputs:
- merged_maps: bfloat16 [128, 7, 7, 768], P('dp', None, None, 'pipe')
- image_grad: float32 [128, 14, 14, 384], P('dp', None, None, 'pipe')
- depth_kernel_grad: float32 [7, 7, 384], replicated
- depth_bias_grad: float32 [384], replicated
- norm_gain_grad: float32 [384], replicated
- norm_shift_grad: float32 [384], replicated
- up_weight_grad: float32 [384, 1536], replicated
- up_bias_grad: float32 [1536], replicated
- down_weight_grad: float32 [1536, 384], replicated
- down_bias_grad: float32 [384], replicated
- layer_scale_grad: float32 [384], replicated
- merge_gain_grad: float32 [384], replicated
- merge_shift_grad: float32 [384], replicated
- patch_weight_grad: float32 [1536, 768], replicated
- patch_bias_grad: float32 [768], replicated
All inputs are finite; a program needn't handle non-finite values. No bound on the sum of `keep_mask` on one device may be relied on, other than what follows from the above.
Results may differ from a plain program's by a relative error of at most 0.0086.
Values may be sent and summed in bfloat16 or wider, within the bound.
A program may use at most 320 MiB of HBM per device.

v0:
```python
import jax
import jax.numpy as jnp
from jax import lax
from jax.sharding import PartitionSpec as P

C = 384
FF = 1536
OUT = 768
SIDE = 14
MICRO = 4
IMG_MICRO = 4
HALF = 7


def for_sending(shard):
    return jax.tree.map(lambda a: a.astype(jnp.bfloat16) if a.dtype == jnp.float32 else a, shard)


def from_behind(block, axis, distance):
    devices = range(lax.axis_size(axis))
    route = [(i - distance, i) for i in devices if i - distance in devices]
    return lax.ppermute(block, axis, route)


def layer_norm(values, gain, shift):
    mean = jnp.mean(values, axis=-1, keepdims=True)
    centered = values - mean
    variance = jnp.mean(centered * centered, axis=-1, keepdims=True)
    return centered * lax.rsqrt(variance + 1e-06) * gain + shift


def depthwise(inputs, kernel, bias):
    height = inputs.shape[1]
    width = inputs.shape[2]
    padded = jnp.pad(inputs, ((0, 0), (3, 3), (3, 3), (0, 0)))
    total = bias + jnp.zeros_like(inputs)
    for across in range(7):
        for down in range(7):
            total = (
                total
                + padded[:, across : across + height, down : down + width, :] * kernel[across, down]
            )
    return total


def first_section(inputs, kernel, bias, gain, shift):
    return layer_norm(depthwise(inputs, kernel, bias), gain, shift)


def gelu_value(value):
    return value * 0.5 * (1.0 + lax.erf(value * 0.7071067811865476))


def gelu_slope(value):
    density = jnp.exp(-0.5 * value * value) * 0.3989422804014327
    return 0.5 * (1.0 + lax.erf(value * 0.7071067811865476)) + value * density


def add_into(grads, updates):
    listed = list(grads)
    for index, value in updates:
        listed[index] = listed[index] + value
    return tuple(listed)


def contract_rows(left, right):
    return lax.dot_general(
        left, right, (((0,), (0,)), ((), ())), preferred_element_type=jnp.float32
    )


def contract_cols(left, right):
    return lax.dot_general(
        left, right, (((1,), (1,)), ((), ())), preferred_element_type=jnp.float32
    )


def shards(
    images,
    depth_kernel,
    depth_bias,
    norm_gain,
    norm_shift,
    up_weight,
    up_bias,
    down_weight,
    down_bias,
    layer_scale,
    merge_gain,
    merge_shift,
    patch_weight,
    patch_bias,
    keep_mask,
    out_grad,
):
    section = lax.axis_index("pipe")
    rows = IMG_MICRO * SIDE * SIDE
    quads = IMG_MICRO * HALF * HALF
    keep_scale = keep_mask.astype(jnp.float32) / 0.9
    zero_narrow = jnp.zeros((rows, C), jnp.bfloat16)
    zero_wide = jnp.zeros((rows, FF), jnp.bfloat16)
    zero_maps = jnp.zeros((IMG_MICRO, HALF, HALF, OUT), jnp.bfloat16)

    def micro_images(slot):
        return lax.dynamic_slice_in_dim(images, slot * IMG_MICRO, IMG_MICRO, 0)

    def micro_factor(slot):
        return jnp.repeat(
            lax.dynamic_slice_in_dim(keep_scale, slot * IMG_MICRO, IMG_MICRO, 0), SIDE * SIDE
        )[:, None]

    def to_patches(values):
        shaped = values.reshape(IMG_MICRO, HALF, 2, HALF, 2, C).transpose(0, 1, 3, 2, 4, 5)
        return shaped.reshape(quads, 4 * C)

    def from_patches(values):
        shaped = values.reshape(IMG_MICRO, HALF, HALF, 2, 2, C).transpose(0, 1, 3, 2, 4, 5)
        return shaped.reshape(rows, C)

    def forward_one(operand):
        slot, narrow_in, wide_in, skip_in = operand
        inputs = micro_images(slot)
        normed = first_section(
            inputs.astype(jnp.float32), depth_kernel, depth_bias, norm_gain, norm_shift
        )
        return (
            normed.astype(jnp.bfloat16).reshape(rows, C),
            zero_wide,
            inputs.reshape(rows, C),
            zero_maps,
        )

    def forward_two(operand):
        slot, narrow_in, wide_in, skip_in = operand
        hidden = jnp.dot(narrow_in, up_weight, preferred_element_type=jnp.float32) + up_bias
        return (zero_narrow, gelu_value(hidden).astype(jnp.bfloat16), skip_in, zero_maps)

    def forward_three(operand):
        slot, narrow_in, wide_in, skip_in = operand
        branch = jnp.dot(wide_in, down_weight, preferred_element_type=jnp.float32) + down_bias
        residual = skip_in.astype(jnp.float32) + micro_factor(slot) * layer_scale * branch
        return (residual.astype(jnp.bfloat16), zero_wide, zero_narrow, zero_maps)

    def forward_four(operand):
        slot, narrow_in, wide_in, skip_in = operand
        normed = layer_norm(narrow_in.astype(jnp.float32), merge_gain, merge_shift).astype(
            jnp.bfloat16
        )
        maps = (
            jnp.dot(to_patches(normed), patch_weight, preferred_element_type=jnp.float32)
            + patch_bias
        )
        return (
            zero_narrow,
            zero_wide,
            zero_narrow,
            maps.astype(jnp.bfloat16).reshape(IMG_MICRO, HALF, HALF, OUT),
        )

    def forward_spare(operand):
        return (zero_narrow, zero_wide, zero_narrow, zero_maps)

    stash_narrow = jnp.zeros((MICRO + 1, rows, C), jnp.bfloat16)
    stash_wide = jnp.zeros((MICRO + 1, rows, FF), jnp.bfloat16)
    maps_store = jnp.zeros((MICRO + 1, IMG_MICRO, HALF, HALF, OUT), jnp.bfloat16)
    narrow_in, wide_in, skip_in = (zero_narrow, zero_wide, zero_narrow)
    for tick in range(MICRO + 3):
        micro = tick - section
        valid = (micro >= 0) & (micro < MICRO)
        slot = jnp.clip(micro, 0, MICRO - 1)
        holder = jnp.where(valid, micro, MICRO)
        branch_index = jnp.where(valid, section, 4)
        narrow_out, wide_out, skip_out, maps = lax.switch(
            branch_index,
            [forward_one, forward_two, forward_three, forward_four, forward_spare],
            (slot, narrow_in, wide_in, skip_in),
        )
        stash_narrow = lax.dynamic_update_index_in_dim(stash_narrow, narrow_in, holder, 0)
        stash_wide = lax.dynamic_update_index_in_dim(stash_wide, wide_in, holder, 0)
        maps_store = lax.dynamic_update_index_in_dim(maps_store, maps, holder, 0)
        if tick < MICRO + 2:
            narrow_in, wide_in, skip_in = (
                from_behind(for_sending(narrow_out), "pipe", 1).astype(narrow_out.dtype),
                from_behind(for_sending(wide_out), "pipe", 1).astype(wide_out.dtype),
                from_behind(for_sending(skip_out), "pipe", 1).astype(skip_out.dtype),
            )
    maps_all = maps_store[:MICRO].reshape(MICRO * IMG_MICRO, HALF, HALF, OUT).astype(jnp.float32)
    merged = lax.psum_scatter(
        maps_all.astype(jnp.bfloat16), "pipe", scatter_dimension=3, tiled=True
    )

    def backward_one(operand):
        slot, narrow_back, wide_back, grads, image_acc = operand
        inputs = micro_images(slot).astype(jnp.float32)
        normed, pull = jax.vjp(
            first_section, inputs, depth_kernel, depth_bias, norm_gain, norm_shift
        )
        input_part, kernel_part, bias_part, gain_part, shift_part = pull(
            narrow_back.astype(jnp.float32).reshape(IMG_MICRO, SIDE, SIDE, C)
        )
        start = slot * IMG_MICRO
        current = lax.dynamic_slice_in_dim(image_acc, start, IMG_MICRO, 0)
        image_acc = lax.dynamic_update_slice_in_dim(image_acc, current + input_part, start, 0)
        grads = add_into(grads, ((0, kernel_part), (1, bias_part), (2, gain_part), (3, shift_part)))
        return (zero_narrow, zero_wide, grads, image_acc)

    def backward_two(operand):
        slot, narrow_back, wide_back, grads, image_acc = operand
        inputs = lax.dynamic_index_in_dim(stash_narrow, slot, 0, keepdims=False)
        hidden = jnp.dot(inputs, up_weight, preferred_element_type=jnp.float32) + up_bias
        hidden_grad = (wide_back.astype(jnp.float32) * gelu_slope(hidden)).astype(jnp.bfloat16)
        weight_part = contract_rows(inputs, hidden_grad)
        bias_part = jnp.sum(hidden_grad.astype(jnp.float32), axis=0)
        input_back = contract_cols(hidden_grad, up_weight).astype(jnp.bfloat16)
        grads = add_into(grads, ((4, weight_part), (5, bias_part)))
        return (input_back, zero_wide, grads, image_acc)

    def backward_three(operand):
        slot, narrow_back, wide_back, grads, image_acc = operand
        activated = lax.dynamic_index_in_dim(stash_wide, slot, 0, keepdims=False)
        branch = jnp.dot(activated, down_weight, preferred_element_type=jnp.float32) + down_bias
        factor = micro_factor(slot)
        upstream = narrow_back.astype(jnp.float32)
        scale_part = jnp.sum(upstream * factor * branch, axis=0)
        branch_grad = (upstream * (factor * layer_scale)).astype(jnp.bfloat16)
        weight_part = contract_rows(activated, branch_grad)
        bias_part = jnp.sum(branch_grad.astype(jnp.float32), axis=0)
        activated_back = contract_cols(branch_grad, down_weight).astype(jnp.bfloat16)
        start = slot * IMG_MICRO
        current = lax.dynamic_slice_in_dim(image_acc, start, IMG_MICRO, 0)
        image_acc = lax.dynamic_update_slice_in_dim(
            image_acc, current + upstream.reshape(IMG_MICRO, SIDE, SIDE, C), start, 0
        )
        grads = add_into(grads, ((6, weight_part), (7, bias_part), (8, scale_part)))
        return (zero_narrow, activated_back, grads, image_acc)

    def backward_four(operand):
        slot, narrow_back, wide_back, grads, image_acc = operand
        residual = lax.dynamic_index_in_dim(stash_narrow, slot, 0, keepdims=False)
        normed, pull = jax.vjp(layer_norm, residual.astype(jnp.float32), merge_gain, merge_shift)
        patches = to_patches(normed.astype(jnp.bfloat16))
        upstream = lax.dynamic_slice_in_dim(out_grad, slot * IMG_MICRO, IMG_MICRO, 0).reshape(
            quads, OUT
        )
        weight_part = contract_rows(patches, upstream)
        bias_part = jnp.sum(upstream.astype(jnp.float32), axis=0)
        patch_back = contract_cols(upstream, patch_weight)
        residual_back, gain_part, shift_part = pull(from_patches(patch_back))
        grads = add_into(
            grads, ((9, gain_part), (10, shift_part), (11, weight_part), (12, bias_part))
        )
        return (residual_back.astype(jnp.bfloat16), zero_wide, grads, image_acc)

    def backward_spare(operand):
        slot, narrow_back, wide_back, grads, image_acc = operand
        return (zero_narrow, zero_wide, grads, image_acc)

    grads = tuple(
        (
            jnp.zeros(item.shape, jnp.float32)
            for item in (
                depth_kernel,
                depth_bias,
                norm_gain,
                norm_shift,
                up_weight,
                up_bias,
                down_weight,
                down_bias,
                layer_scale,
                merge_gain,
                merge_shift,
                patch_weight,
                patch_bias,
            )
        )
    )
    image_acc = jnp.zeros((MICRO * IMG_MICRO, SIDE, SIDE, C), jnp.float32)
    narrow_back, wide_back = (zero_narrow, zero_wide)
    for tick in range(MICRO + 3):
        micro = tick + section - 3
        valid = (micro >= 0) & (micro < MICRO)
        slot = jnp.clip(micro, 0, MICRO - 1)
        branch_index = jnp.where(valid, section, 4)
        narrow_send, wide_send, grads, image_acc = lax.switch(
            branch_index,
            [backward_one, backward_two, backward_three, backward_four, backward_spare],
            (slot, narrow_back, wide_back, grads, image_acc),
        )
        if tick < MICRO + 2:
            returned = from_behind(
                for_sending(jnp.pad(narrow_send, ((0, 0), (0, FF - C))) + wide_send), "pipe", -1
            )
            narrow_back, wide_back = (returned[:, :C], returned)
    image_grad = jax.tree.map(
        lambda part: part.astype(jnp.float32),
        lax.psum_scatter(for_sending(image_acc), "pipe", scatter_dimension=3, tiled=True),
    )
    summed = lax.psum(
        (
            grads[0],
            grads[1],
            grads[2],
            grads[3],
            grads[4],
            grads[5],
            grads[6],
            grads[7],
            grads[8],
            grads[9],
            grads[10],
            grads[11],
            grads[12],
        ),
        ("pipe", "dp"),
    )
    return (
        merged,
        image_grad,
        summed[0],
        summed[1],
        summed[2],
        summed[3],
        summed[4],
        summed[5],
        summed[6],
        summed[7],
        summed[8],
        summed[9],
        summed[10],
        summed[11],
        summed[12],
    )


def solution(mesh):
    placed = (
        P("dp", None, None, None),
        P(),
        P(),
        P(),
        P(),
        P(),
        P(),
        P(),
        P(),
        P(),
        P(),
        P(),
        P(),
        P(),
        P("dp"),
        P("dp", None, None, None),
    )
    return jax.shard_map(
        shards,
        mesh=mesh,
        in_specs=placed,
        out_specs=(
            P("dp", None, None, "pipe"),
            P("dp", None, None, "pipe"),
            P(),
            P(),
            P(),
            P(),
            P(),
            P(),
            P(),
            P(),
            P(),
            P(),
            P(),
            P(),
            P(),
        ),
        check_vma=False,
    )
```

profile of v0, /device:TPU:1, one launch (start us, length us, event | category | flops | bytes accessed | tf_op | source)
XLA Modules:
  0.0 1795.2 jit_solution(3332309309253630406)
XLA Ops:
  8.7 24.7 %conditional.14 = (bf16[784,384]{1,0:T(8,128)(2,1)}, bf16[784,1536]{1,0:T(8,128)(2,1)}, bf16[784,384]{1,0:T(8,128)(2,1)S(1)}, bf16[1,4,7,7,768]{4,1,0,3,2:T(4,128)(2,1)S(1)}) conditional(s32[]{:T(128)} %clamp.42, (f32[384]{0:T(512)}, s32[]{:T(128)}, bf16[16,14,14,384]{3,0,2,1:T(8,128)(2,1)}, f32[7,7,384]{2,1,0:T(8,128)}, ...), branch_computations={%region_0.3_spmd, %region_3.4_spmd, %region_4.5_spmd, %region_5.6_... | conditional | flops 932069376 | bytes 18039530 | solution.py:173
  38.9 61.0 %collective-permute-done = bf16[784,384]{1,0:T(8,128)(2,1)S(1)} collective-permute-done((bf16[784,384]{1,0:T(8,128)(2,1)}, bf16[784,384]{1,0:T(8,128)(2,1)S(1)}, u32[]{:S(2)}, u32[]{:S(2)}) %collective-permute-start) | collective-permute-done | bytes 602144 | tf_op jit(solution)/shard_map/ppermute | solution.py:22
  112.7 26.5 %conditional.15 = (bf16[784,384]{1,0:T(8,128)(2,1)S(1)}, bf16[784,1536]{1,0:T(8,128)(2,1)}, bf16[784,384]{1,0:T(8,128)(2,1)S(1)}, bf16[1,4,7,7,768]{4,1,0,3,2:T(4,128)(2,1)S(1)}) conditional(s32[]{:T(128)} %clamp.43, (f32[384]{0:T(512)}, s32[]{:T(128)}, bf16[16,14,14,384]{3,0,2,1:T(8,128)(2,1)}, ...), branch_computations={%region_7.0_spmd, %region_10.11_spmd, %region_11.12_spmd, %region_... | conditional | flops 932069376 | bytes 18039530 | solution.py:173
  145.4 59.5 %collective-permute-done.3 = bf16[784,384]{1,0:T(8,128)(2,1)S(1)} collective-permute-done((bf16[784,384]{1,0:T(8,128)(2,1)S(1)}, bf16[784,384]{1,0:T(8,128)(2,1)S(1)}, u32[]{:S(2)}, u32[]{:S(2)}) %collective-permute-start.3) | collective-permute-done | bytes 602144 | tf_op jit(solution)/shard_map/ppermute | solution.py:22
  217.8 36.3 %conditional.16 = (bf16[784,384]{1,0:T(8,128)(2,1)S(1)}, bf16[784,1536]{1,0:T(8,128)(2,1)}, bf16[784,384]{1,0:T(8,128)(2,1)}, bf16[1,4,7,7,768]{4,1,0,3,2:T(4,128)(2,1)S(1)}) conditional(s32[]{:T(128)} %clamp.44, (f32[384]{0:T(512)}, s32[]{:T(128)}, bf16[16,14,14,384]{3,0,2,1:T(8,128)(2,1)}, f32[7,7,384]{2,1,0:T(8,128)}, ...), branch_computations={%region_16.19_spmd, %region_19.20_spmd, %region_20.21_spmd, %regio... | conditional | flops 932069376 | bytes 20448006 | solution.py:173
  260.3 58.9 %collective-permute-done.6 = bf16[784,384]{1,0:T(8,128)(2,1)S(1)} collective-permute-done((bf16[784,384]{1,0:T(8,128)(2,1)S(1)}, bf16[784,384]{1,0:T(8,128)(2,1)S(1)}, u32[]{:S(2)}, u32[]{:S(2)}) %collective-permute-start.6) | collective-permute-done | bytes 602144 | tf_op jit(solution)/shard_map/ppermute | solution.py:22
  332.2 27.5 %conditional.17 = (bf16[784,384]{1,0:T(8,128)(2,1)S(1)}, bf16[784,1536]{1,0:T(8,128)(2,1)}, bf16[784,384]{1,0:T(8,128)(2,1)}, bf16[1,4,7,7,768]{4,1,0,3,2:T(4,128)(2,1)S(1)}) conditional(s32[]{:T(128)} %clamp.45, (f32[384]{0:T(512)}, s32[]{:T(128)}, bf16[16,14,14,384]{3,0,2,1:T(8,128)(2,1)}, f32[7,7,384]{2,1,0:T(8,128)}, ...), branch_computations={%region_25.28_spmd, %region_28.29_spmd, %region_29.30_spmd, %regio... | conditional | flops 932069376 | bytes 20448006 | solution.py:173
  366.1 58.1 %collective-permute-done.9 = bf16[784,384]{1,0:T(8,128)(2,1)S(1)} collective-permute-done((bf16[784,384]{1,0:T(8,128)(2,1)S(1)}, bf16[784,384]{1,0:T(8,128)(2,1)S(1)}, u32[]{:S(2)}, u32[]{:S(2)}) %collective-permute-start.9) | collective-permute-done | bytes 602144 | tf_op jit(solution)/shard_map/ppermute | solution.py:22
  472.4 37.4 %collective-permute-done.12 = bf16[784,384]{1,0:T(8,128)(2,1)S(1)} collective-permute-done((bf16[784,384]{1,0:T(8,128)(2,1)}, bf16[784,384]{1,0:T(8,128)(2,1)S(1)}, u32[]{:S(2)}, u32[]{:S(2)}) %collective-permute-start.12) | collective-permute-done | bytes 602144 | tf_op jit(solution)/shard_map/ppermute | solution.py:22
  548.3 43.6 %collective-permute-done.15 = bf16[784,384]{1,0:T(8,128)(2,1)S(1)} collective-permute-done((bf16[784,384]{1,0:T(8,128)(2,1)S(1)}, bf16[784,384]{1,0:T(8,128)(2,1)S(1)}, u32[]{:S(2)}, u32[]{:S(2)}) %collective-permute-start.15) | collective-permute-done | bytes 602144 | tf_op jit(solution)/shard_map/ppermute | solution.py:22
  594.5 26.3 %conditional.21 = (bf16[784,1536]{1,0:T(8,128)(2,1)}, f32[7,7,384]{2,1,0:T(8,128)S(1)}, f32[384]{0:T(512)S(1)}, f32[384]{0:T(512)S(1)}, f32[384]{0:T(512)S(1)}, ...) conditional(s32[]{:T(128)} %clamp.55, (s32[]{:T(128)}, ...), branch_computations={%region_60.116_spmd, %region_116.118_spmd, %region_118.121_spmd, %... | conditional | flops 2790486528 | bytes 221175104 | solution.py:285
  626.7 53.9 %collective-permute-done.17 = bf16[784,1536]{1,0:T(8,128)(2,1)} collective-permute-done((bf16[784,1536]{1,0:T(8,128)(2,1)}, bf16[784,1536]{1,0:T(8,128)(2,1)}, u32[]{:S(2)}, u32[]{:S(2)}) %collective-permute-start.17) | collective-permute-done | bytes 2408480 | tf_op jit(solution)/shard_map/ppermute | solution.py:22
  706.2 51.0 %collective-permute-done.18 = bf16[784,1536]{1,0:T(8,128)(2,1)} collective-permute-done((bf16[784,1536]{1,0:T(8,128)(2,1)}, bf16[784,1536]{1,0:T(8,128)(2,1)}, u32[]{:S(2)}, u32[]{:S(2)}) %collective-permute-start.18) | collective-permute-done | bytes 2408480 | tf_op jit(solution)/shard_map/ppermute | solution.py:22
  783.0 107.1 %collective-permute-done.19 = bf16[784,1536]{1,0:T(8,128)(2,1)} collective-permute-done((bf16[784,1536]{1,0:T(8,128)(2,1)}, bf16[784,1536]{1,0:T(8,128)(2,1)}, u32[]{:S(2)}, u32[]{:S(2)}) %collective-permute-start.19) | collective-permute-done | bytes 2408480 | tf_op jit(solution)/shard_map/ppermute | solution.py:22
  891.3 107.1 %conditional.24 = (bf16[784,1536]{1,0:T(8,128)(2,1)}, f32[7,7,384]{2,1,0:T(8,128)S(1)}, f32[384]{0:T(512)}, f32[384]{0:T(512)}, f32[384]{0:T(512)}, /*index=5*/f...) conditional(s32[]{:T(128)} %clamp.52, (s32[]{:T(128)}, ...), branch_computations={%region_272.329_spmd, %region_329.331_spmd, %region_331.334_spmd, ... | conditional | flops 2792282112 | bytes 219304672 | solution.py:285
  951.5 21.4 %pad_add_fusion.22 = f32[4,20,20,384]{3,2,1,0:T(8,128)S(1)} fusion(f32[4,14,14,384]{3,2,1,0:T(8,128)} %get-tuple-element.5302, f32[4,14,14,384]{3,2,1,0:T(8,128)} %get-tuple-element.5303, f32[4,14,14,384]{3,2,1,0:T(8,128)} %get-tuple-element.5304, f32[4,14,14,384]{3,2,1,0:T(8,128)} %get-tuple-element.5305, f32[4,14,14,384]{3,2,1,0:T(8,128)} %get-tuple-element.5306, ...), kind=kLoop, calls=%fused_computation.2411 | loop fusion | flops 25804800 | bytes 54239232 | tf_op jit(solution)/shard_map/cond/branch_0_fun/transpose(jvp())/add_any | solution.py:41
  1004.1 49.0 %collective-permute-done.20 = bf16[784,1536]{1,0:T(8,128)(2,1)} collective-permute-done((bf16[784,1536]{1,0:T(8,128)(2,1)}, bf16[784,1536]{1,0:T(8,128)(2,1)}, u32[]{:S(2)}, u32[]{:S(2)}) %collective-permute-start.20) | collective-permute-done | bytes 2408480 | tf_op jit(solution)/shard_map/ppermute | solution.py:22
  1054.3 105.6 %conditional.25 = (bf16[784,1536]{1,0:T(8,128)(2,1)}, f32[7,7,384]{2,1,0:T(8,128)}, f32[384]{0:T(512)}, f32[384]{0:T(512)}, f32[384]{0:T(512)}, /*index=5*/f32[3...) conditional(s32[]{:T(128)} %clamp.51, (s32[]{:T(128)}, ...), branch_computations={%region_343.400_spmd, %region_400.402_spmd, %region_402.405_spmd, ... | conditional | flops 2792282112 | bytes 219304672 | solution.py:285
  1170.4 43.5 %collective-permute-done.21 = bf16[784,1536]{1,0:T(8,128)(2,1)} collective-permute-done((bf16[784,1536]{1,0:T(8,128)(2,1)}, bf16[784,1536]{1,0:T(8,128)(2,1)}, u32[]{:S(2)}, u32[]{:S(2)}) %collective-permute-start.21) | collective-permute-done | bytes 2408480 | tf_op jit(solution)/shard_map/ppermute | solution.py:22
  1215.0 105.3 %conditional.26 = (bf16[784,1536]{1,0:T(8,128)(2,1)}, f32[7,7,384]{2,1,0:T(8,128)}, f32[384]{0:T(512)}, f32[384]{0:T(512)}, f32[384]{0:T(512)}, /*index=5*/f32[3...) conditional(s32[]{:T(128)} %clamp.50, (s32[]{:T(128)}, ...), branch_computations={%region_414.471_spmd, %region_471.473_spmd, %region_473.476_spmd, ... | conditional | flops 2792282112 | bytes 220085888 | solution.py:285
  1374.7 95.2 %conditional.27 = ((f32[7,7,384]{2,1,0:T(8,128)S(1)}, f32[384]{0:T(512)S(1)}, f32[384]{0:T(512)S(1)}, f32[384]{0:T(512)S(1)}, f32[384,1536]{1,0:T(8,128)}, /*ind...) conditional(s32[]{:T(128)} %clamp.49, (s32[]{:T(128)}, ...), branch_computations={%region_485.542_spmd, %region_542.544_spmd, %region_544.547_spmd, ... | conditional | flops 1867137024 | bytes 209564416 | solution.py:285
  1493.4 23.4 %reshape.3461 = bf16[384,3136]{1,0:T(8,128)(2,1)} reshape(bf16[384,14,14,16]{3,2,1,0:T(8,128)(2,1)} %bitcast.447) | data formatting | bytes 4816896
  1525.7 70.1 %all-reduce.729 = (f32[384]{0:T(512)}, f32[384]{0:T(512)}, f32[384]{0:T(512)}, f32[1536]{0:T(1024)}, f32[384]{0:T(512)}, /*index=5*/f32[384]{0:T(512)}, f32[384]{0:T(512)}, f32[384]{0:T(512)}, f32[768]{0:T(1024)}) all-reduce(f32[384]{0:T(512)S(1)} %get-tuple-element.2422, ...), channel_id=1, replica_groups=mesh['pipe'=4,'dp'=8] {'pipe','dp'}, use_global_device_ids=true, to_apply=%region_556.557 | all-reduce | flops 4992 | bytes 39936 | tf_op jit(solution)/shard_map/psum | solution.py:299
  1621.3 156.0 %all-reduce.733.cloned.1.call-done = (f32[7,7,384]{2,1,0:T(8,128)}, f32[384,1536]{1,0:T(8,128)}, f32[1536,384]{1,0:T(8,128)}, f32[1536,768]{1,0:T(8,128)}) async-done(((f32[7,7,384]{2,1,0:T(8,128)}, f32[384,1536]{1,0:T(8,128)}, f32[1536,384]{1,0:T(8,128)}, f32[1536,768]{1,0:T(8,128)}), (f32[7,7,384]{2,1,0:T(8,128)}, f32[384,1536]{1,0:T(8,128)}, f32[1536,384]{1,0:T(8,128)}, ...) | async-done | bytes 9512464 | tf_op jit(solution)/shard_map/psum | solution.py:299
  (909 shorter events, 805.0 us)
Async XLA Ops:
  8.0 1509.4 %reduce-scatter.7.cloned.1.call-start = ((), (), s32[]{:S(2)}) async-start(), calls=%async_computation.2 | async-start | bytes 1720320
  33.5 79.2 %collective-permute-start.2 = (bf16[784,1536]{1,0:T(8,128)(2,1)}, bf16[784,1536]{1,0:T(8,128)(2,1)}, u32[]{:S(2)}, u32[]{:S(2)}) collective-permute-start(bf16[784,1536]{1,0:T(8,128)(2,1)} %get-tuple-element.2304), channel_id=1, source_target_pairs={{0,8},{8,16},{16,24},{1,9},{9,17},{17,25},{2,10},{10,18},{18,26},{... | collective-permute-start | bytes 7225352 | tf_op jit(solution)/shard_map/ppermute | solution.py:22
  36.2 63.7 %collective-permute-start = (bf16[784,384]{1,0:T(8,128)(2,1)}, bf16[784,384]{1,0:T(8,128)(2,1)S(1)}, u32[]{:S(2)}, u32[]{:S(2)}) collective-permute-start(bf16[784,384]{1,0:T(8,128)(2,1)} %get-tuple-element.2302), channel_id=1, source_target_pairs={{0,8},{8,16},{16,24},{1,9},{9,17},{17,25},{2,10},{10,18},{18,26},{... | collective-permute-start | bytes 1806344 | tf_op jit(solution)/shard_map/ppermute | solution.py:22
  37.5 75.2 %collective-permute-start.1 = (bf16[784,384]{1,0:T(8,128)(2,1)S(1)}, bf16[784,384]{1,0:T(8,128)(2,1)S(1)}, u32[]{:S(2)}, u32[]{:S(2)}) collective-permute-start(bf16[784,384]{1,0:T(8,128)(2,1)S(1)} %get-tuple-element.2303), channel_id=1, source_target_pairs={{0,8},{8,16},{16,24},{1,9},{9,17},{17,25},{2,10},{10,18},{18,26},{... | collective-permute-start | bytes 1806344 | tf_op jit(solution)/shard_map/ppermute | solution.py:22
  139.2 78.6 %collective-permute-start.5 = (bf16[784,1536]{1,0:T(8,128)(2,1)}, bf16[784,1536]{1,0:T(8,128)(2,1)}, u32[]{:S(2)}, u32[]{:S(2)}) collective-permute-start(bf16[784,1536]{1,0:T(8,128)(2,1)} %get-tuple-element.2308), channel_id=1, source_target_pairs={{0,8},{8,16},{16,24},{1,9},{9,17},{17,25},{2,10},{10,18},{18,26},{... | collective-permute-start | bytes 7225352 | tf_op jit(solution)/shard_map/ppermute | solution.py:22
  141.9 63.0 %collective-permute-start.3 = (bf16[784,384]{1,0:T(8,128)(2,1)S(1)}, bf16[784,384]{1,0:T(8,128)(2,1)S(1)}, u32[]{:S(2)}, u32[]{:S(2)}) collective-permute-start(bf16[784,384]{1,0:T(8,128)(2,1)S(1)} %get-tuple-element.2306), channel_id=1, source_target_pairs={{0,8},{8,16},{16,24},{1,9},{9,17},{17,25},{2,10},{10,18},{18,26},{... | collective-permute-start | bytes 1806344 | tf_op jit(solution)/shard_map/ppermute | solution.py:22
  143.3 74.5 %collective-permute-start.4 = (bf16[784,384]{1,0:T(8,128)(2,1)S(1)}, bf16[784,384]{1,0:T(8,128)(2,1)}, u32[]{:S(2)}, u32[]{:S(2)}) collective-permute-start(bf16[784,384]{1,0:T(8,128)(2,1)S(1)} %get-tuple-element.2307), channel_id=1, source_target_pairs={{0,8},{8,16},{16,24},{1,9},{9,17},{17,25},{2,10},{10,18},{18,26},{... | collective-permute-start | bytes 1806344 | tf_op jit(solution)/shard_map/ppermute | solution.py:22
  254.1 78.1 %collective-permute-start.8 = (bf16[784,1536]{1,0:T(8,128)(2,1)}, bf16[784,1536]{1,0:T(8,128)(2,1)}, u32[]{:S(2)}, u32[]{:S(2)}) collective-permute-start(bf16[784,1536]{1,0:T(8,128)(2,1)} %get-tuple-element.2312), channel_id=1, source_target_pairs={{0,8},{8,16},{16,24},{1,9},{9,17},{17,25},{2,10},{10,18},{18,26},{... | collective-permute-start | bytes 7225352 | tf_op jit(solution)/shard_map/ppermute | solution.py:22
  256.8 62.4 %collective-permute-start.6 = (bf16[784,384]{1,0:T(8,128)(2,1)S(1)}, bf16[784,384]{1,0:T(8,128)(2,1)S(1)}, u32[]{:S(2)}, u32[]{:S(2)}) collective-permute-start(bf16[784,384]{1,0:T(8,128)(2,1)S(1)} %get-tuple-element.2310), channel_id=1, source_target_pairs={{0,8},{8,16},{16,24},{1,9},{9,17},{17,25},{2,10},{10,18},{18,26},{... | collective-permute-start | bytes 1806344 | tf_op jit(solution)/shard_map/ppermute | solution.py:22
  258.2 74.0 %collective-permute-start.7 = (bf16[784,384]{1,0:T(8,128)(2,1)}, bf16[784,384]{1,0:T(8,128)(2,1)}, u32[]{:S(2)}, u32[]{:S(2)}) collective-permute-start(bf16[784,384]{1,0:T(8,128)(2,1)} %get-tuple-element.2311), channel_id=1, source_target_pairs={{0,8},{8,16},{16,24},{1,9},{9,17},{17,25},{2,10},{10,18},{18,26},{... | collective-permute-start | bytes 1806344 | tf_op jit(solution)/shard_map/ppermute | solution.py:22
  359.8 77.5 %collective-permute-start.11 = (bf16[784,1536]{1,0:T(8,128)(2,1)}, bf16[784,1536]{1,0:T(8,128)(2,1)}, u32[]{:S(2)}, u32[]{:S(2)}) collective-permute-start(bf16[784,1536]{1,0:T(8,128)(2,1)} %get-tuple-element.2316), channel_id=1, source_target_pairs={{0,8},{8,16},{16,24},{1,9},{9,17},{17,25},{2,10},{10,18},{18,26},{... | collective-permute-start | bytes 7225352 | tf_op jit(solution)/shard_map/ppermute | solution.py:22
  362.6 61.6 %collective-permute-start.9 = (bf16[784,384]{1,0:T(8,128)(2,1)S(1)}, bf16[784,384]{1,0:T(8,128)(2,1)S(1)}, u32[]{:S(2)}, u32[]{:S(2)}) collective-permute-start(bf16[784,384]{1,0:T(8,128)(2,1)S(1)} %get-tuple-element.2314), channel_id=1, source_target_pairs={{0,8},{8,16},{16,24},{1,9},{9,17},{17,25},{2,10},{10,18},{18,26},{... | collective-permute-start | bytes 1806344 | tf_op jit(solution)/shard_map/ppermute | solution.py:22
  364.0 73.3 %collective-permute-start.10 = (bf16[784,384]{1,0:T(8,128)(2,1)}, bf16[784,384]{1,0:T(8,128)(2,1)}, u32[]{:S(2)}, u32[]{:S(2)}) collective-permute-start(bf16[784,384]{1,0:T(8,128)(2,1)} %get-tuple-element.2315), channel_id=1, source_target_pairs={{0,8},{8,16},{16,24},{1,9},{9,17},{17,25},{2,10},{10,18},{18,26},{... | collective-permute-start | bytes 1806344 | tf_op jit(solution)/shard_map/ppermute | solution.py:22
  439.9 82.7 %collective-permute-start.14 = (bf16[784,1536]{1,0:T(8,128)(2,1)}, bf16[784,1536]{1,0:T(8,128)(2,1)}, u32[]{:S(2)}, u32[]{:S(2)}) collective-permute-start(bf16[784,1536]{1,0:T(8,128)(2,1)} %get-tuple-element.2320), channel_id=1, source_target_pairs={{0,8},{8,16},{16,24},{1,9},{9,17},{17,25},{2,10},{10,18},{18,26},{... | collective-permute-start | bytes 7225352 | tf_op jit(solution)/shard_map/ppermute | solution.py:22
  465.8 56.8 %collective-permute-start.13 = (bf16[784,384]{1,0:T(8,128)(2,1)S(1)}, bf16[784,384]{1,0:T(8,128)(2,1)}, u32[]{:S(2)}, u32[]{:S(2)}) collective-permute-start(bf16[784,384]{1,0:T(8,128)(2,1)S(1)} %copy-done.125), channel_id=1, source_target_pairs={{0,8},{8,16},{16,24},{1,9},{9,17},{17,25},{2,10},{10,18},{18,26},{... | collective-permute-start | bytes 1806344 | tf_op jit(solution)/shard_map/ppermute | solution.py:22
  526.2 66.7 %collective-permute-start.16 = (bf16[784,1536]{1,0:T(8,128)(2,1)}, bf16[784,1536]{1,0:T(8,128)(2,1)S(1)}, u32[]{:S(2)}, u32[]{:S(2)}) collective-permute-start(bf16[784,1536]{1,0:T(8,128)(2,1)} %get-tuple-element.2323), channel_id=1, source_target_pairs={{0,8},{8,16},{16,24},{1,9},{9,17},{17,25},{2,10},{10,18},{18,26},{... | collective-permute-start | bytes 7225352 | tf_op jit(solution)/shard_map/ppermute | solution.py:22
  539.1 52.8 %collective-permute-start.15 = (bf16[784,384]{1,0:T(8,128)(2,1)S(1)}, bf16[784,384]{1,0:T(8,128)(2,1)S(1)}, u32[]{:S(2)}, u32[]{:S(2)}) collective-permute-start(bf16[784,384]{1,0:T(8,128)(2,1)S(1)} %copy-done.126), channel_id=1, source_target_pairs={{0,8},{8,16},{16,24},{1,9},{9,17},{17,25},{2,10},{10,18},{18,26},{... | collective-permute-start | bytes 1806344 | tf_op jit(solution)/shard_map/ppermute | solution.py:22
  625.4 55.2 %collective-permute-start.17 = (bf16[784,1536]{1,0:T(8,128)(2,1)}, bf16[784,1536]{1,0:T(8,128)(2,1)}, u32[]{:S(2)}, u32[]{:S(2)}) collective-permute-start(bf16[784,1536]{1,0:T(8,128)(2,1)} %add.4793), channel_id=1, source_target_pairs={{8,0},{16,8},{24,16},{9,1},{17,9},{25,17},{10,2},{18,10},{26,18},{... | collective-permute-start | bytes 7225352 | tf_op jit(solution)/shard_map/ppermute | solution.py:22
  704.9 52.3 %collective-permute-start.18 = (bf16[784,1536]{1,0:T(8,128)(2,1)}, bf16[784,1536]{1,0:T(8,128)(2,1)}, u32[]{:S(2)}, u32[]{:S(2)}) collective-permute-start(bf16[784,1536]{1,0:T(8,128)(2,1)} %add.4794), channel_id=1, source_target_pairs={{8,0},{16,8},{24,16},{9,1},{17,9},{25,17},{10,2},{18,10},{26,18},{... | collective-permute-start | bytes 7225352 | tf_op jit(solution)/shard_map/ppermute | solution.py:22
  781.7 108.4 %collective-permute-start.19 = (bf16[784,1536]{1,0:T(8,128)(2,1)}, bf16[784,1536]{1,0:T(8,128)(2,1)}, u32[]{:S(2)}, u32[]{:S(2)}) collective-permute-start(bf16[784,1536]{1,0:T(8,128)(2,1)} %add.4795), channel_id=1, source_target_pairs={{8,0},{16,8},{24,16},{9,1},{17,9},{25,17},{10,2},{18,10},{26,18},{... | collective-permute-start | bytes 7225352 | tf_op jit(solution)/shard_map/ppermute | solution.py:22
  1002.8 50.3 %collective-permute-start.20 = (bf16[784,1536]{1,0:T(8,128)(2,1)}, bf16[784,1536]{1,0:T(8,128)(2,1)}, u32[]{:S(2)}, u32[]{:S(2)}) collective-permute-start(bf16[784,1536]{1,0:T(8,128)(2,1)} %add.4796), channel_id=1, source_target_pairs={{8,0},{16,8},{24,16},{9,1},{17,9},{25,17},{10,2},{18,10},{26,18},{... | collective-permute-start | bytes 7225352 | tf_op jit(solution)/shard_map/ppermute | solution.py:22
  1164.4 49.5 %collective-permute-start.21 = (bf16[784,1536]{1,0:T(8,128)(2,1)}, bf16[784,1536]{1,0:T(8,128)(2,1)}, u32[]{:S(2)}, u32[]{:S(2)}) collective-permute-start(bf16[784,1536]{1,0:T(8,128)(2,1)} %add.4797), channel_id=1, source_target_pairs={{8,0},{16,8},{24,16},{9,1},{17,9},{25,17},{10,2},{18,10},{26,18},{... | collective-permute-start | bytes 7225352 | tf_op jit(solution)/shard_map/ppermute | solution.py:22
  1361.2 244.5 %reduce-scatter.9.cloned.1.call-start = ((), (), s32[]{:S(2)}) async-start(), calls=%async_computation.3 | async-start | bytes 3072000
  1516.8 260.4 %all-reduce.733.cloned.1.call-start = ((), (), s32[]{:S(2)}) async-start(), calls=%async_computation.4 | async-start | bytes 19046400 | tf_op jit(solution)/shard_map/psum | solution.py:299
  (205 other events, 3479.4 us)
Sparse Core Ops, SparseCore 0:
  1361.3 42.1 reduce-scatter.6
  1517.0 88.6 reduce-scatter.8
Sparse Core Ops, SparseCore 1:
  1526.0 251.1 all-reduce.732
where the time goes:
time: 1810 us; the launch traced here: 1800 us
  waiting for transfers between devices  866 us (48%)
  other arithmetic  406 us (22%)
  local copies, waits for them, and re-layouts  257 us (14%)
  loops' own time  123 us (7%)
  blocking collectives  70.1 us (4%)
  starting transfers between devices  55.6 us (3%)
    ppermute x23, waiting for transfers between devices, from_behind(): return lax.ppermute(block, axis, route)  700 us
    psum x1, waiting for transfers between devices, shards(): lax.psum((grads[0], grads[1], grads[2], grads[3], grads[4], grads[5], gra...  156 us
    another operation x7, loops' own time, shards(): lax.switch(branch_index, [backward_one, backward_two, backward_three, bac...  113 us
    unnamed x138, local copies, waits for them, and re-layouts  106 us
    mul x16, other arithmetic, depthwise(): padded[:, across:across + height, down:down + width, :]  105 us
    reduce_sum x8, other arithmetic, layer_norm(): mean = jnp.mean(values, axis=-1, keepdims=True)  98.6 us
    add_any x4, other arithmetic, depthwise(): padded[:, across:across + height, down:down + width, :]  84.9 us
    psum x1, blocking collectives, shards(): lax.psum((grads[0], grads[1], grads[2], grads[3], grads[4], grads[5], gra...  70.1 us
  transfers between devices with their start and end apart: 26, of which 19 were waited for; matrix products, arithmetic and copies ran while one was open for 12% of the time, Pallas kernels for 0%

commit v1 on v0

v1 whole, which is shorter than its diff:
```python
import functools
from types import SimpleNamespace

import jax
import jax.numpy as jnp
import numpy as np
from jax import lax
from jax.experimental import pallas as pl
from jax.experimental.pallas import tpu as pltpu
from jax.sharding import PartitionSpec as P

C = 384
FF = 1536
OUT = 768
SIDE = 14
WIDE = 16
HALF = 7
RING = SIDE + 3
FREQ = 160
SPEC = 2 * FREQ
MAP = SIDE * WIDE
CELLS = HALF * 8
TAPS = 56
SMALL = 64
F32 = jnp.float32
BF16 = jnp.bfloat16


def split_matrix(matrix):
    high = matrix.astype(BF16)
    low = (matrix - high.astype(np.float64)).astype(BF16)
    return high, low


def transforms():
    pairs = [(0, 0)] + [(u, 0) for u in range(1, 9)] + [(u, v) for v in range(1, 9) for u in range(RING)]
    freq = np.zeros((FREQ, 2))
    freq[: len(pairs)] = np.array(pairs)
    live = (np.arange(FREQ) < len(pairs)).astype(np.float64)
    weight = np.where(np.arange(FREQ) == 0, 1.0, 2.0) * live
    plain = np.array([(h, w, w < SIDE) for h in range(SIDE) for w in range(WIDE)])
    cell = np.array(
        [(h, 2 * b + j, b < HALF) for h in range(SIDE) for j in range(2) for b in range(8)]
    )
    taps = np.array([(i - 3, j - 3, j < 7) for i in range(7) for j in range(8)])

    def angles(places):
        return 2 * np.pi / RING * (freq @ places[:, :2].T)

    def forward(places, sign):
        turn = angles(places)
        scale = places[:, 2][None, :] * live[:, None] / RING
        return np.concatenate([np.cos(turn) * scale, sign * np.sin(turn) * scale], 0)

    def backward(places):
        turn = angles(places).T
        scale = places[:, 2][:, None] * weight[None, :] / RING
        return np.concatenate([np.cos(turn) * scale, -np.sin(turn) * scale], 1)

    move = np.zeros((MAP, MAP))
    for row, (h, w, ok) in enumerate(cell):
        if ok:
            move[row, h * WIDE + w] = 1.0
    in_high, in_low = split_matrix(forward(plain, -1.0))
    spread = np.concatenate([move, 0.0 * move], 1).astype(BF16)
    from_plain = np.concatenate([np.concatenate([in_high, in_low], 1), spread], 0)
    cell_high, cell_low = split_matrix(forward(cell, -1.0))
    from_cell = np.concatenate([cell_high, cell_low, cell_high], 1)
    high, low = split_matrix(backward(cell))
    to_cell = np.concatenate([high, high, low], 1)
    high, low = split_matrix(backward(plain))
    to_plain = np.concatenate([high, high, low, move.T.astype(BF16)], 1)
    high, low = split_matrix(forward(taps, 1.0) * RING)
    from_taps = np.concatenate([high, high, low], 1)
    high, low = split_matrix(backward(taps) * RING)
    to_taps = np.concatenate([high, high, low], 1)
    return from_plain, from_cell, to_cell, to_plain, from_taps, to_taps


def dot(left, right):
    return jnp.dot(left, right, preferred_element_type=F32)


def dot_rows(left, right):
    return lax.dot_general(left, right, (((0,), (0,)), ((), ())), preferred_element_type=F32)


def dot_cols(left, right):
    return lax.dot_general(left, right, (((1,), (1,)), ((), ())), preferred_element_type=F32)


def two_parts(value):
    high = value.astype(BF16)
    return high, (value - high.astype(F32)).astype(BF16)


def mean_of(value):
    return jnp.sum(value, axis=-1, keepdims=True) * (1.0 / C)


def fold(value):
    rows = value.shape[0]
    total = value[0:8]
    for at in range(8, rows, 8):
        total = total + value[at : at + 8]
    return total


def gelu_parts(value):
    below = 1.0 + jnp.abs(value) * (0.3275911 * 0.7071067811865476)
    t = pl.reciprocal(below, approx=True)
    t = t * (2.0 - below * t)
    bell = jnp.exp2(value * value * (-0.5 * 1.4426950408889634))
    tail = 0.5 * 1.061405429 * t - 0.5 * 1.453152027
    tail = tail * t + 0.5 * 1.421413741
    tail = tail * t - 0.5 * 0.284496736
    tail = tail * t + 0.5 * 0.254829592
    tail = tail * (t * bell)
    area = jnp.where(value >= 0.0, 1.0 - tail, tail)
    return value * area, area + value * (bell * 0.3989422804014327)


def alternate(steps, product, work, buffers):
    first, second = buffers
    product(0, first)

    def both(i, carry):
        product(2 * i + 1, second)
        carry = work(2 * i, first, carry)
        product(jnp.minimum(2 * i + 2, steps - 1), first)
        return work(2 * i + 1, second, carry)

    return functools.partial(lax.fori_loop, 0, steps // 2, both)


def put_split(store, rows, lanes, value):
    high, low = two_parts(value)
    at, count = rows
    store[pl.ds(at, count), lanes] = high
    store[pl.ds(SPEC + at, count), lanes] = low
    store[pl.ds(2 * SPEC + at, count), lanes] = high


def compute(own, first_image, keep_of, refs, grads, maps_out, image_out, small, s, at_point):
    (taps_in, kbias, gain1, shift1, bup, bdown, scale, gain2, shift2, bpatch, from_taps) = refs
    x, og, up, down, wpatch = s.x, s.og, s.up, s.down, s.wpatch
    from_cell, to_plain, to_taps = s.from_cell, s.to_plain, s.to_taps
    from_plain, to_cell = s.from_plain, s.to_cell
    pairs = own // 2
    groups = own * HALF

    def row(ref):
        return ref[...].reshape(1, -1)

    s.taps[...] = jnp.zeros((TAPS, C), F32)
    for i in range(7):
        s.taps[i * 8 : i * 8 + 7, :] = taps_in[i]
    high, low = two_parts(s.taps[...])
    s.khat[...] = dot(from_taps[...], jnp.concatenate([high, low, high], 0))

    at_point("og")
    images = s.x_in.shape[2]

    def take(a, carry):
        for b in range(HALF):
            v = s.og_in[a, b].astype(F32)
            for k in range(6):
                at = (8 * k + b) * images
                s.line[at : at + images, :] = v[:, k * 128 : k * 128 + 128]
        for n in range(own):
            at = pl.multiple_of((n * HALF + a) * 8, 8)
            for k in range(6):
                v = s.line[pl.ds(8 * k * images + first_image + n, 8, stride=images), :]
                s.maps[pl.ds(at, 8), k * 128 : k * 128 + 128] = v
        return carry

    for k in range(6):
        s.line[(8 * k + HALF) * images : (8 * k + 8) * images, :] = jnp.zeros((images, 128), F32)
    lax.fori_loop(0, HALF, take, 0)
    og[...] = s.maps[...].astype(BF16)

    at_point("x")
    plane = WIDE * images

    def widen(h, carry):
        for w in range(SIDE):
            v = s.x_in[h, w].astype(F32)
            for k in range(3):
                s.line[k * plane + w * images : k * plane + w * images + images, :] = v[:, k * 128 : k * 128 + 128]
        for n in range(own):
            for k in range(3):
                v = s.line[pl.ds(k * plane + first_image + n, WIDE, stride=images), :]
                x[n, pl.ds(pl.multiple_of(h * WIDE, WIDE), WIDE), k * 128 : k * 128 + 128] = v.astype(BF16)
        return carry

    for k in range(3):
        s.line[k * plane + SIDE * images : k * plane + plane, :] = jnp.zeros(((WIDE - SIDE) * images, 128), F32)
    lax.fori_loop(0, SIDE, widen, 0, unroll=2)

    bias_row, g1, s1 = row(kbias), row(gain1), row(shift1)

    at_point("f")

    def first(pair, carry):
        both = jnp.concatenate([x[2 * pair], x[2 * pair + 1]], 1)
        s.spec[pair] = dot(from_plain[:SPEC, :], jnp.concatenate([both, both], 0))
        s.moved[pair] = dot(from_plain[SPEC:, :MAP], both)

        def product(t, carry):
            at = pl.multiple_of(t * 16, 16)
            kre, kim = s.khat[pl.ds(at, 16), :], s.khat[pl.ds(FREQ + at, 16), :]
            for half in range(2):
                lanes = slice(half * C, half * C + C)
                re, im = s.spec[pair, pl.ds(at, 16), lanes], s.spec[pair, pl.ds(FREQ + at, 16), lanes]
                put_split(s.wave, (at, 16), lanes, re * kre - im * kim)
                put_split(s.wave, (FREQ + at, 16), lanes, im * kre + re * kim)
            return carry

        lax.fori_loop(0, FREQ // 16, product, 0, unroll=2)
        s.conv[...] = dot(to_cell[...], s.wave[: 3 * SPEC, :])

        def norm(t, carry):
            for half in range(2):
                for k in range(2):
                    at = pl.multiple_of(t * 32 + k * 16, 16)
                    v = s.conv[pl.ds(at, 16), half * C : half * C + C] + bias_row
                    v = v - mean_of(v)
                    r = lax.rsqrt(mean_of(v * v) + 1e-06)
                    n = v * r
                    to = pl.multiple_of((2 * pair + half) * MAP + at, 16)
                    s.n1[pl.ds(to, 16), :] = n
                    s.r1[pl.ds(to, 16), :] = r
                    s.normed[pl.ds(to, 16), :] = (n * g1 + s1).astype(BF16)
            return carry

        lax.fori_loop(0, MAP // 32, norm, 0, unroll=True)
        return carry

    lax.fori_loop(0, pairs, first, 0)

    wide = FF // 2
    block = 2 * MAP

    some = MAP // 2
    blocks = own * MAP // some

    def rows_of(k):
        return pl.ds(pl.multiple_of(k * some, 16), some)

    def expand(part):
        lanes = slice(part * wide, part * wide + wide)
        bias = row(bup)[:, lanes]

        def product(k, target):
            target[...] = dot(s.normed[rows_of(k), :], up[:, lanes])

        def curve(k, source, carry):
            for at in range(0, some, 16):
                to = pl.multiple_of(k * some + at, 16)
                for lane in range(0, wide, 256):
                    v = source[at : at + 16, lane : lane + 256] + bias[:, lane : lane + 256]
                    value, slope = gelu_parts(v)
                    s.act[part, pl.ds(to, 16), lane : lane + 256] = value.astype(BF16)
                    s.slope[part, pl.ds(to, 16), lane : lane + 256] = slope
            return carry

        alternate(blocks, product, curve, (s.hidden, s.hidden_too))(0)

    at_point("up")
    for part in range(2):
        expand(part)
    at_point("down")

    def reduce(pair, carry):
        rows = pl.ds(pl.multiple_of(pair * block, block), block)
        s.branch[rows, :] = (
            dot(s.act[0, rows, :], down[:wide, :]) + dot(s.act[1, rows, :], down[wide:, :]) + row(bdown)
        )
        return carry

    lax.fori_loop(0, pairs, reduce, 0)

    ls, g2, s2 = row(scale), row(gain2), row(shift2)

    def join(t, carry):
        for i in range(2):
            pieces = []
            for k in range(2):
                group = 4 * t + 2 * i + k
                factor = keep_of(group // HALF)
                at = pl.multiple_of(group * 32, 32)
                inside = pl.multiple_of((group % HALF) * 32, 32)
                image = group // HALF
                lane = pl.ds(pl.multiple_of((image % 2) * C, C), C)
                v = s.moved[image // 2, pl.ds(inside, 32), lane]
                v = v + factor * ls * s.branch[pl.ds(at, 32), :]
                v = v.astype(BF16).astype(F32)
                v = v - mean_of(v)
                r = lax.rsqrt(mean_of(v * v) + 1e-06)
                n = v * r
                s.n2[pl.ds(at, 32), :] = n
                s.r2[pl.ds(at, 32), :] = r
                pieces.append(n * g2 + s2)
            to = pl.multiple_of(t * 32 + i * 16, 16)
            for ij in range(4):
                both = jnp.concatenate([piece[ij * 8 : ij * 8 + 8] for piece in pieces], 0)
                s.patches[pl.ds(to, 16), ij * C : ij * C + C] = both.astype(BF16)
        return carry

    lax.fori_loop(0, groups // 4, join, 0)

    for ij in range(4):
        g = dot_rows(s.patches[:, ij * C : ij * C + C], og[...])
        grads[0, ij * C : ij * C + C, :] = g[:, :C].astype(BF16)
        grads[1, ij * C : ij * C + C, :] = g[:, C:].astype(BF16)
        if ij == 1:
            at_point("p0")
    at_point("p1")

    s.maps[...] = dot(s.patches[...], wpatch[...]) + row(bpatch)
    count = maps_out.shape[0]
    part = OUT // count

    def share(t, carry):
        at = pl.multiple_of(t * 16, 16)
        v = s.maps[pl.ds(at, 16), :]
        for q in range(count):
            turned = v if q == 0 else pltpu.roll(v, OUT - q * part, 1)
            maps_out[q, pl.ds(at, 16), :] = turned[:, :part].astype(BF16)
        return carry

    lax.fori_loop(0, own * CELLS // 16, share, 0, unroll=2)
    at_point("m")

    s.back[...] = dot_cols(og[...], wpatch[...])
    at_point("b")

    zero = jnp.zeros((8, C), F32)

    def unjoin(t, carry):
        for k in range(2):
            sum_gain, sum_shift, sum_scale, sum_bias = carry
            group = 2 * t + k
            factor = keep_of(group // HALF)
            from_row = pl.multiple_of(group * 8, 8)
            at = pl.multiple_of(group * 32, 32)
            m = s.back[pl.ds(from_row, 8), :]
            m = jnp.concatenate([m[:, ij * C : ij * C + C] for ij in range(4)], 0)
            n = s.n2[pl.ds(at, 32), :]
            sum_gain = sum_gain + fold(m * n)
            sum_shift = sum_shift + fold(m)
            e = m * g2
            back = s.r2[pl.ds(at, 32), :] * (e - mean_of(e) - n * mean_of(e * n))
            low = back.astype(BF16)
            back = low.astype(F32)
            image = group // HALF
            inside = pl.multiple_of((group % HALF) * 32, 32)
            s.rgrad[image, pl.ds(inside, 32), :] = low
            sum_scale = sum_scale + fold(back * s.branch[pl.ds(at, 32), :]) * factor
            bg = back * (factor * ls)
            s.bgrad[pl.ds(at, 32), :] = bg.astype(BF16)
            sum_bias = sum_bias + fold(bg)
            carry = sum_gain, sum_shift, sum_scale, sum_bias
        return carry

    sums = lax.fori_loop(0, groups // 4, unjoin, (zero,) * 4)
    at_point("j0")
    sum_gain, sum_shift, sum_scale, sum_bias = lax.fori_loop(groups // 4, groups // 2, unjoin, sums)
    for k, total in ((31, sum_bias), (39, sum_scale), (47, sum_gain), (55, sum_shift)):
        s.rows[k // 8 : k // 8 + 1, :] = jnp.sum(total, 0, keepdims=True)
    at_point("j")

    for part in range(2):
        g = dot_rows(s.act[part], s.bgrad[...])
        grads[2, part * wide : part * wide + wide, :] = g.astype(BF16)
        at_point("d0" if part == 0 else "d1")

    def slopes(part):
        def product(k, target):
            target[...] = dot_cols(s.bgrad[rows_of(k), :], down[part * wide : part * wide + wide, :])

        def times(k, source, carry):
            carry = list(carry)
            for at in range(0, some, 16):
                to = pl.multiple_of(k * some + at, 16)
                for i, lane in enumerate(range(0, wide, C)):
                    v = source[at : at + 16, lane : lane + C] * s.slope[part, pl.ds(to, 16), lane : lane + C]
                    s.act[part, pl.ds(to, 16), lane : lane + C] = v.astype(BF16)
                    carry[i] = carry[i] + fold(v)
            return tuple(carry)

        a, b = alternate(blocks, product, times, (s.hidden, s.hidden_too))((zero, zero))
        s.usum[part * 16 : part * 16 + 8, :] = a
        s.usum[part * 16 + 8 : part * 16 + 16, :] = b

    for part in range(2):
        slopes(part)
        at_point("s" + str(2 * part + 1))

    for part in range(2):
        g = dot_rows(s.normed[...], s.act[part])
        grads[3, 2 * part * C : 2 * part * C + C, :] = g[:, :C].astype(BF16)
        grads[3, 2 * part * C + C : 2 * part * C + 2 * C, :] = g[:, C:].astype(BF16)
        at_point("u0" if part == 0 else "u1")

    def narrow(pair, carry):
        rows = pl.ds(pl.multiple_of(pair * block, block), block)
        s.branch[rows, :] = dot_cols(s.act[0, rows, :], up[:, :wide]) + dot_cols(s.act[1, rows, :], up[:, wide:])
        return carry

    for pair in range(pairs):
        narrow(pair, 0)
        at_point("n0" if pair < pairs - 1 else "n")

    s.zhat[...] = jnp.zeros((SPEC, C), F32)

    def last(pair, carry):
        def unnorm(t, carry):
            for half in range(2):
                sum_gain, sum_shift, sum_bias = carry
                at = pl.multiple_of(t * 32, 32)
                to = pl.multiple_of((2 * pair + half) * MAP + at, 32)
                m = s.branch[pl.ds(to, 32), :]
                n = s.n1[pl.ds(to, 32), :]
                sum_gain = sum_gain + fold(m * n)
                sum_shift = sum_shift + fold(m)
                e = m * g1
                back = s.r1[pl.ds(to, 32), :] * (e - mean_of(e) - n * mean_of(e * n))
                sum_bias = sum_bias + fold(back)
                high, low = two_parts(back)
                lanes = slice(half * C, half * C + C)
                s.chigh[pl.ds(at, 32), lanes] = high
                s.clow[pl.ds(at, 32), lanes] = low
                s.wave[pl.ds(3 * SPEC + at, 32), lanes] = s.rgrad[2 * pair + half, pl.ds(at, 32), :]
                carry = sum_gain, sum_shift, sum_bias
            return carry

        carry = lax.fori_loop(0, MAP // 32, unnorm, carry, unroll=True)
        at_point("l" + str(3 * pair))
        high = s.chigh[...]
        s.ghat[...] = dot(from_cell[...], jnp.concatenate([high, high, s.clow[...]], 0))
        at_point("l" + str(3 * pair + 1))

        def product(t, carry):
            at = pl.multiple_of(t * 16, 16)
            kre, kim = s.khat[pl.ds(at, 16), :], s.khat[pl.ds(FREQ + at, 16), :]
            zre, zim = s.zhat[pl.ds(at, 16), :], s.zhat[pl.ds(FREQ + at, 16), :]
            for half in range(2):
                lanes = slice(half * C, half * C + C)
                re, im = s.ghat[pl.ds(at, 16), lanes], s.ghat[pl.ds(FREQ + at, 16), lanes]
                xre, xim = s.spec[pair, pl.ds(at, 16), lanes], s.spec[pair, pl.ds(FREQ + at, 16), lanes]
                zre = zre + re * xre + im * xim
                zim = zim + re * xim - im * xre
                put_split(s.wave, (at, 16), lanes, re * kre + im * kim)
                put_split(s.wave, (FREQ + at, 16), lanes, im * kre - re * kim)
            s.zhat[pl.ds(at, 16), :] = zre
            s.zhat[pl.ds(FREQ + at, 16), :] = zim
            return carry

        lax.fori_loop(0, FREQ // 16, product, 0, unroll=2)
        s.moved[pair] = dot(to_plain[...], s.wave[...])
        return carry

    carry = (zero,) * 3
    for pair in range(pairs):
        carry = last(pair, carry)
        at_point("l" + str(3 * pair + 2))
    sum_gain, sum_shift, sum_bias = carry

    def pack(t, carry):
        at = pl.multiple_of(t * 16, 16)
        lanes = lax.broadcasted_iota(jnp.int32, (16, C), 1)
        values = [s.moved[n // 2, pl.ds(at, 16), (n % 2) * C : (n % 2) * C + C] for n in range(own)]
        size = C // count
        for q in range(count):
            total = None
            for n in range(own):
                turn = ((n - q) * size) % C
                v = values[n] if turn == 0 else pltpu.roll(values[n], turn, 1)
                total = v if total is None else jnp.where(lanes >= n * size, v, total)
            image_out[q, pl.ds(at, 16), :] = total.astype(BF16)
        return carry

    lax.fori_loop(0, MAP // 16, pack, 0)
    at_point("i")

    zhigh, zlow = two_parts(s.zhat[...])
    small[0:TAPS, :] = dot(to_taps[...], jnp.concatenate([zhigh, zlow, zhigh], 0))
    small[7:8, :] = jnp.sum(sum_bias, 0, keepdims=True)
    small[15:16, :] = jnp.sum(sum_gain, 0, keepdims=True)
    small[23:24, :] = jnp.sum(sum_shift, 0, keepdims=True)
    for k in range(3, 7):
        small[8 * k + 7 : 8 * k + 8, :] = s.rows[k : k + 1, :]
    for k in range(4):
        small[56 + k : 57 + k, :] = jnp.sum(s.usum[k * 8 : k * 8 + 8, :], 0, keepdims=True)
    ones = fold(og[...].astype(F32))
    ones = jnp.sum(ones, 0, keepdims=True)
    small[60:61, :] = ones[:, :C]
    small[61:62, :] = ones[:, C:]
    small[62:64, :] = jnp.zeros((2, C), F32)
    at_point("t")


def scratch(own, ways, groups):
    count = own * ways
    steps = sum(groups_of(groups, ways), [])
    sum_rows, sum_copies = landing(2 * C, 16, steps)
    small_rows, small_copies = landing(SMALL, SMALL // 2, steps)
    rows = own * MAP
    pairs = own // 2
    return dict(
        x_in=pltpu.VMEM((SIDE, SIDE, count, C), BF16),
        line=pltpu.VMEM((3 * WIDE * count, 128), F32),
        x=pltpu.VMEM((own, MAP, C), BF16),
        og_in=pltpu.VMEM((HALF, HALF, count, OUT), BF16),
        og=pltpu.VMEM((own * CELLS, OUT), BF16),
        up=pltpu.VMEM((C, FF), BF16),
        down=pltpu.VMEM((FF, C), BF16),
        wpatch=pltpu.VMEM((4 * C, OUT), BF16),
        from_cell=pltpu.VMEM((SPEC, 3 * MAP), BF16),
        to_plain=pltpu.VMEM((MAP, 3 * SPEC + MAP), BF16),
        to_taps=pltpu.VMEM((TAPS, 3 * SPEC), BF16),
        in_sem=pltpu.SemaphoreType.DMA((10,)),
        from_plain=pltpu.VMEM((SPEC + MAP, 2 * MAP), BF16),
        to_cell=pltpu.VMEM((MAP, 3 * SPEC), BF16),
        taps=pltpu.VMEM((TAPS, C), F32),
        khat=pltpu.VMEM((SPEC, C), F32),
        spec=pltpu.VMEM((pairs, SPEC, 2 * C), F32),
        moved=pltpu.VMEM((pairs, MAP, 2 * C), F32),
        wave=pltpu.VMEM((3 * SPEC + MAP, 2 * C), BF16),
        conv=pltpu.VMEM((MAP, 2 * C), F32),
        n1=pltpu.VMEM((rows, C), F32),
        r1=pltpu.VMEM((rows, 1), F32),
        normed=pltpu.VMEM((rows, C), BF16),
        hidden=pltpu.VMEM((MAP // 2, FF // 2), F32),
        hidden_too=pltpu.VMEM((MAP // 2, FF // 2), F32),
        act=pltpu.VMEM((2, rows, FF // 2), BF16),
        slope=pltpu.VMEM((2, rows, FF // 2), F32),
        branch=pltpu.VMEM((rows, C), F32),
        n2=pltpu.VMEM((rows, C), F32),
        r2=pltpu.VMEM((rows, 1), F32),
        patches=pltpu.VMEM((own * CELLS, 4 * C), BF16),
        maps=pltpu.VMEM((own * CELLS, OUT), F32),
        back=pltpu.VMEM((own * CELLS, 4 * C), F32),
        rgrad=pltpu.VMEM((own, MAP, C), BF16),
        bgrad=pltpu.VMEM((rows, C), BF16),
        usum=pltpu.VMEM((32, C), F32),
        rows=pltpu.VMEM((8, C), F32),
        zhat=pltpu.VMEM((SPEC, C), F32),
        ghat=pltpu.VMEM((SPEC, 2 * C), F32),
        chigh=pltpu.VMEM((MAP, 2 * C), BF16),
        clow=pltpu.VMEM((MAP, 2 * C), BF16),
        grads=pltpu.VMEM((4, 4 * C, C), BF16),
        land=pltpu.VMEM((8, sum_rows, C), BF16),
        small=pltpu.VMEM((SMALL, C), F32),
        small_land=pltpu.VMEM((small_rows, C), F32),
        maps_out=pltpu.VMEM((ways, own * CELLS, OUT // ways), BF16),
        maps_in=pltpu.VMEM((ways, own * CELLS, OUT // ways), BF16),
        maps_held=pltpu.VMEM((ways, own * CELLS, -(-OUT // ways // 128) * 128), F32),
        image_out=pltpu.VMEM((ways, MAP, C), BF16),
        sum_send=pltpu.SemaphoreType.DMA((8, sum_copies)),
        sum_recv=pltpu.SemaphoreType.DMA((8, sum_copies)),
        small_send=pltpu.SemaphoreType.DMA((small_copies,)),
        small_recv=pltpu.SemaphoreType.DMA((small_copies,)),
        maps_send=pltpu.SemaphoreType.DMA((ways,)),
        maps_recv=pltpu.SemaphoreType.DMA((ways,)),
        image_send=pltpu.SemaphoreType.DMA((ways,)),
        image_recv=pltpu.SemaphoreType.DMA((ways,)),
    )


def landing(rows, least, steps):
    total, copies = 0, 0
    for at, bits in enumerate(steps):
        ways = 2**bits
        halving = rows % (ways * least) == 0 and at < len(steps) - 1
        rows = rows // ways if halving else rows
        total += (ways - 1) * rows
        copies += 2 * (ways - 1)
    return total, copies


class Sum:
    def __init__(self, work, land, total, rows, least, steps, sems):
        self.work, self.land, self.total = work, land, total
        self.steps, self.sems, self.least = steps, sems, least
        self.at, self.rows, self.start, self.used = 0, rows, 0, 0
        self.copies, self.path, self.slots, self.came = [], [], [], []
        self.count, self.halving, self.gathering = 0, True, False

    def send(self, source, target, axis, partner):
        copy = pltpu.make_async_remote_copy(
            src_ref=source,
            dst_ref=target,
            send_sem=self.sems[0].at[self.count],
            recv_sem=self.sems[1].at[self.count],
            device_id={axis: partner},
            device_id_type=pl.DeviceIdType.MESH,
        )
        copy.start()
        self.count += 1
        self.copies.append(copy)
        self.came.append(copy)

    def add(self, target, start, slots, rows):
        step = self.least
        while step < 64 and rows % (2 * step) == 0:
            step *= 2

        def one(t, carry):
            to = pl.ds(pl.multiple_of(start + t * step, self.least), step)
            total = self.work[to, :]
            for slot in slots:
                total = total + self.land[pl.ds(pl.multiple_of(slot + t * step, self.least), step), :]
            target[to, :] = total
            return carry

        lax.fori_loop(0, rows // step, one, 0)

    def reduce(self):
        start, rows, slots = self.start, self.rows, self.slots
        if self.came:
            for copy in self.came:
                copy.wait_recv()
            self.at += 1
            if self.at == len(self.steps):
                self.add(self.total, start, slots, rows)
                self.gather()
                return
            if not self.halving:
                for copy in self.came:
                    copy.wait_send()
                self.copies = self.copies[: len(self.copies) - len(self.came)]
        axis, index, bits = self.steps[self.at]
        ways = 2 ** len(bits)
        self.halving = rows % (ways * self.least) == 0 and self.at < len(self.steps) - 1
        count = rows // ways if self.halving else rows
        if slots and not self.halving:
            self.add(self.work, start, slots, rows)
        self.slots, self.came = [], []
        for mask in range(1, ways):
            partner, block = index, 0
            for k, (bit, delta) in enumerate(bits):
                away = mask >> k & 1
                partner = partner + away * delta
                block = block + (1 - bit if away else bit) * 2**k
            give = count * block if self.halving else 0
            if slots and self.halving:
                self.add(self.work, start + give, [slot + give for slot in slots], count)
            source = self.work.at[pl.ds(pl.multiple_of(start + give, self.least), count), :]
            self.send(source, self.land.at[pl.ds(self.used, count), :], axis, partner)
            self.slots.append(self.used)
            self.used += count
        keep = 0
        if self.halving:
            keep = count * sum(bit * 2**k for k, (bit, _) in enumerate(bits))
            self.path.append((axis, index, bits, start, rows))
            if slots:
                self.add(self.work, start + keep, [slot + keep for slot in slots], count)
        self.start, self.rows = start + keep, count

    def gather(self):
        self.gathering, self.came = True, []
        if self.path:
            axis, index, bits, start, rows = self.path.pop()
            here = self.total.at[pl.ds(pl.multiple_of(self.start, self.least), self.rows), :]
            for mask in range(1, 2 ** len(bits)):
                partner = index
                for k, (_, delta) in enumerate(bits):
                    partner = partner + (mask >> k & 1) * delta
                self.send(here, here, axis, partner)
            self.start, self.rows = start, rows

    def go(self):
        if not self.gathering:
            self.reduce()
        elif self.came:
            for copy in self.came:
                copy.wait_recv()
            self.gather()

    def running(self):
        return not self.gathering or bool(self.came)

    def finish(self):
        for copy in self.copies:
            copy.wait_send()


PARTS = ((0, 0), (1, 0), (0, 768), (1, 768), (2, 0), (2, 768), (3, 0), (3, 768))
IMAGE, MAPS = 100, 101
SCHEDULE = {
    "p0": (0,),
    "p1": (3,),
    "b": (0,),
    "j0": (2, MAPS, 1),
    "j": (3,),
    "d1": (5, 4, 2, 1),
    "s1": (0,),
    "u0": (6, 5, 3, 0),
    "u1": (4,),
    "n": (2, 1, 7, 3, 0, 6),
    "l2": (5, 7),
    "l3": (3, 0, 1),
    "l4": (2,),
    "l5": (6, 5, 3),
    "t": (8, 1, 4, 6),
    "end": (7, 8, 2, 0, 1, 5, 4, 3, 6, 7, 2, 8, 5, IMAGE, 4, 1, 3, 0, 6, 7, 1, 8, 4, 2, 5, 7, 6, 2, 4, 8, 7, 4, 8, 6, 5, 7),
}


def groups_of(groups, ways):
    left = groups.bit_length() - 1
    near = [1] if left else []
    left -= len(near)
    while left:
        near.append(min(2, left))
        left -= near[-1]
    return near, [1] * (ways.bit_length() - 1)


def routes(groups, ways):
    def steps(axis, sizes):
        index, stride, found = lax.axis_index(axis), 1, []
        for size in sizes:
            bits = []
            for _ in range(size):
                bit = lax.rem(lax.div(index, stride), 2)
                bits.append((bit, stride * (1 - 2 * bit)))
                stride *= 2
            found.append((axis, index, bits))
        return found

    near, far = groups_of(groups, ways)
    return steps("dp", near), steps("pipe", far)


def unpack_maps(own, ways, low, held, tall, cells):
    part, count = low.shape[2], own * ways

    def hold(t, carry):
        rows = pl.ds(pl.multiple_of(t * 16, 16), 16)
        for q in range(ways):
            held[q, rows, :part] = low[q, rows, :].astype(F32)
        return carry

    def unmap(a, carry):
        for lane in range(0, part, 128):
            for q in range(ways):
                for n in range(own):
                    v = held[q, pl.ds(pl.multiple_of((n * HALF + a) * 8, 8), 8), lane : lane + 128]
                    tall[pl.ds(lane // 128 * 8 * count + q * own + n, 8, stride=count), :] = v
            for b in range(HALF):
                at = lane // 128 * 8 * count + b * count
                v = tall[at : at + count, : min(128, part - lane)]
                cells[a, b, :, lane : min(lane + 128, part)] = v.astype(BF16)
        return carry

    lax.fori_loop(0, own * CELLS // 16, hold, 0)
    lax.fori_loop(0, HALF, unmap, 0)


def exchange(ways, source, land, sems):
    p = lax.axis_index("pipe")
    copies = []
    for j in range(1, ways):
        q = lax.rem(p + j, ways)
        copy = pltpu.make_async_remote_copy(
            src_ref=source.at[q],
            dst_ref=land.at[p],
            send_sem=sems[0].at[j - 1],
            recv_sem=sems[1].at[j - 1],
            device_id={"pipe": q},
            device_id_type=pl.DeviceIdType.MESH,
        )
        copy.start()
        copies.append(copy)
    return copies


def whole_kernel(own, ways, groups, *refs):
    keep = refs[0]
    ins = refs[1:12]
    images, out_grad, up, down, wpatch, from_cell, to_plain, to_taps, from_plain, to_cell = refs[12:22]
    total, maps_all, image_in, small_total = refs[22:26]
    s = SimpleNamespace(**dict(zip(scratch(own, ways, groups), refs[26:])))
    p = lax.axis_index("pipe")
    start = p * own
    fetched = {}
    for k, (name, source, target) in enumerate(
        (
            ("g", out_grad, s.og_in),
            ("x", images, s.x_in),
            ("f", from_plain, s.from_plain),
            ("e", to_cell, s.to_cell),
            ("u", up, s.up),
            ("d", down, s.down),
            ("w", wpatch, s.wpatch),
            ("c", from_cell, s.from_cell),
            ("p", to_plain, s.to_plain),
            ("t", to_taps, s.to_taps),
        )
    ):
        fetched[name] = pltpu.make_async_copy(source, target, s.in_sem.at[k])
        fetched[name].start()

    def keep_of(image):
        return keep[start + image].astype(F32) / 0.9

    near, far = routes(groups, ways)
    barrier = pltpu.get_barrier_semaphore()
    met = [("pipe", lax.rem(p + j, ways)) for j in range(1, ways)]
    for axis, index, bits in near:
        for mask in range(1, 2 ** len(bits)):
            met.append((axis, index + sum((mask >> k & 1) * delta for k, (_, delta) in enumerate(bits))))
    for axis, partner in met:
        pl.semaphore_signal(barrier, inc=1, device_id={axis: partner}, device_id_type=pl.DeviceIdType.MESH)

    steps = near + far

    def part_sum(i, k, first):
        rows = pl.ds(first, 2 * C)

        return Sum(
            s.grads.at[k, rows, :], s.land.at[i], total.at[k, rows, :], 2 * C, 16, steps,
            (s.sum_send.at[i], s.sum_recv.at[i]),
        )

    sums = [part_sum(i, k, first) for i, (k, first) in enumerate(PARTS)]
    tail = Sum(
        s.small, s.small_land, small_total, SMALL, SMALL // 2, steps, (s.small_send, s.small_recv)
    )
    chains = sums + [tail]
    kept = {}
    needs = {"og": "g", "x": "x", "f": "fe", "up": "u", "down": "d", "p0": "w", "n": "cpt"}

    def at_point(name):
        for needed in needs.get(name, ""):
            fetched[needed].wait()
        if name == "p0":
            pl.semaphore_wait(barrier, len(met))
        if name == "l4":
            for copy in kept[MAPS]:
                copy.wait_recv()
            unpack_maps(own, ways, s.maps_in, s.maps_held, s.line, maps_all)
        for k in SCHEDULE.get(name, ()):
            if k == MAPS:
                kept[k] = exchange(ways, s.maps_out, s.maps_in, (s.maps_send, s.maps_recv))
                s.maps_in[p] = s.maps_out[p]
            elif k == IMAGE:
                kept[k] = exchange(ways, s.image_out, image_in, (s.image_send, s.image_recv))
                image_in[p] = s.image_out[p]
            else:
                chains[k].go()

    compute(own, start, keep_of, ins, s.grads, s.maps_out, s.image_out, s.small, s, at_point)
    at_point("end")
    while any(chain.running() for chain in chains):
        for chain in chains:
            if chain.running():
                chain.go()
    exchanged = kept[MAPS] + kept[IMAGE]
    for copy in kept[IMAGE]:
        copy.wait_recv()
    for copy in exchanged:
        copy.wait_send()
    for chain in chains:
        chain.finish()


def whole_call(own, ways, groups, args):
    vmem = pl.BlockSpec(memory_space=pltpu.VMEM)
    away = pl.BlockSpec(memory_space=pl.ANY)
    return pl.pallas_call(
        functools.partial(whole_kernel, own, ways, groups),
        out_shape=(
            pltpu.VMEM((4, 4 * C, C), BF16),
            pltpu.VMEM((HALF, HALF, own * ways, OUT // ways), BF16),
            pltpu.VMEM((ways, MAP, C), BF16),
            jax.ShapeDtypeStruct((SMALL, C), F32),
        ),
        in_specs=[pl.BlockSpec(memory_space=pltpu.SMEM)] + [vmem] * 11 + [away] * 10,
        out_specs=[vmem] * 4,
        scratch_shapes=list(scratch(own, ways, groups).values()),
        compiler_params=pltpu.CompilerParams(
            collective_id=0, has_side_effects=True, vmem_limit_bytes=57 * 2**20
        ),
    )(*args)


def finish_kernel(own, ways, grads, maps, image, small, *refs):
    (merged, image_grad, taps, kbias, gain1, shift1, up_grad, up_bias, down_grad, down_bias, scale, gain2,
     shift2, patch_grad, patch_bias, patches, downs, ups, images, tall, sems) = refs
    size, count = C // ways, own * ways

    def block(c):
        return pl.ds(c * C, C)

    sent = []

    def send(source, target):
        copy = pltpu.make_async_copy(source, target, sems.at[len(sent)])
        copy.start()
        sent.append(copy)

    def widen(k, c, target, row, lane):
        def step(t, carry):
            at = t * 32
            target[pl.ds(pl.multiple_of(row + at, 32), 32), lane : lane + C] = grads[
                k, pl.ds(pl.multiple_of(c * C + at, 32), 32), :
            ].astype(F32)
            return carry

        lax.fori_loop(0, C // 32, step, 0, unroll=4)

    def patch(c):
        widen(0, c, patches, c * C, 0)
        widen(1, c, patches, c * C, C)
        send(patches.at[block(c), :], patch_grad.at[block(c), :])

    send(maps, merged)

    def unpack(h, carry):
        for q in range(ways):
            v = image[q, pl.ds(pl.multiple_of(h * WIDE, WIDE), WIDE), :].astype(F32)
            for n in range(own):
                first = n * size // 128 * 128
                turn = v[:, first : min(first + 256, C)]
                if n * size > first:
                    turn = pltpu.roll(turn, turn.shape[1] - (n * size - first), 1)
                tall[pl.ds(q * own + n, WIDE, stride=count), :] = turn[:, :128]
        for w in range(SIDE):
            images[h, w] = tall[w * count : w * count + count, :size]
        return carry

    for c in range(2):
        patch(c)
        rows = pl.ds(c * HALF, HALF)
        lax.fori_loop(c * HALF, c * HALF + HALF, unpack, 0)
        send(images.at[rows], image_grad.at[rows])
    patch(2)
    patch(3)
    for c in range(4):
        widen(2, c, downs, c * C, 0)
        if c % 2:
            rows = pl.ds((c - 1) * C, 2 * C)
            send(downs.at[rows, :], down_grad.at[rows, :])
    for c in range(4):
        widen(3, c, ups, 0, c * C)
        if c % 2:
            lanes = pl.ds((c - 1) * C, 2 * C)
            send(ups.at[:, lanes], up_grad.at[:, lanes])
    for i in range(7):
        taps[i] = small[i * 8 : i * 8 + 7, :]
    for i, out in enumerate((kbias, gain1, shift1, down_bias, scale, gain2, shift2)):
        out[...] = small[i * 8 + 7 : i * 8 + 8, :].reshape(C)
    for k in range(4):
        up_bias[k * C : k * C + C] = small[TAPS + k : TAPS + k + 1, :].reshape(C)
    for k in range(2):
        patch_bias[k * C : k * C + C] = small[TAPS + 4 + k : TAPS + 5 + k, :].reshape(C)
    for copy in sent:
        copy.wait()


def finish_call(own, ways, grads, maps, image, small):
    count = ways * own
    size, part = C // ways, OUT // ways
    vector = jax.ShapeDtypeStruct((C,), F32)
    shapes = (
        jax.ShapeDtypeStruct((HALF, HALF, count, part), BF16),
        jax.ShapeDtypeStruct((SIDE, SIDE, count, size), F32),
        jax.ShapeDtypeStruct((7, 7, C), F32),
        vector,
        vector,
        vector,
        jax.ShapeDtypeStruct((C, FF), F32),
        jax.ShapeDtypeStruct((FF,), F32),
        jax.ShapeDtypeStruct((FF, C), F32),
        vector,
        vector,
        vector,
        vector,
        jax.ShapeDtypeStruct((4 * C, OUT), F32),
        jax.ShapeDtypeStruct((OUT,), F32),
    )
    away = pl.BlockSpec(memory_space=pl.ANY)
    near = pl.BlockSpec(memory_space=pltpu.VMEM)
    outs = pl.pallas_call(
        functools.partial(finish_kernel, own, ways),
        out_shape=shapes,
        in_specs=[near] * 4,
        out_specs=[away if k in (0, 1, 6, 8, 13) else near for k in range(15)],
        scratch_shapes=[
            pltpu.VMEM((4 * C, OUT), F32),
            pltpu.VMEM((FF, C), F32),
            pltpu.VMEM((C, FF), F32),
            pltpu.VMEM((SIDE, SIDE, count, size), F32),
            pltpu.VMEM((WIDE * count, 128), F32),
            pltpu.SemaphoreType.DMA((32,)),
        ],
        compiler_params=pltpu.CompilerParams(vmem_limit_bytes=50 * 2**20),
    )(*[pltpu.with_memory_space_constraint(v, pltpu.VMEM) for v in (grads, maps, image)], small)
    return (outs[0].transpose(2, 0, 1, 3), outs[1].transpose(2, 0, 1, 3)) + tuple(outs[2:])


def shards(
    images, depth_kernel, depth_bias, norm_gain, norm_shift, up_weight, up_bias, down_weight, down_bias,
    layer_scale, merge_gain, merge_shift, patch_weight, patch_bias, keep_mask, out_grad,
):
    ways = lax.axis_size("pipe")
    own = images.shape[0] // ways
    from_plain, from_cell, to_cell, to_plain, from_taps, to_taps = [jnp.asarray(m) for m in transforms()]
    packed = whole_call(
        own, ways, lax.axis_size("dp"),
        (keep_mask, depth_kernel, depth_bias, norm_gain, norm_shift, up_bias, down_bias, layer_scale,
         merge_gain, merge_shift, patch_bias, from_taps,
         images.transpose(1, 2, 0, 3), out_grad.transpose(1, 2, 0, 3), up_weight, down_weight, patch_weight,
         from_cell, to_plain, to_taps, from_plain, to_cell),
    )
    return finish_call(own, ways, *packed)


def solution(mesh):
    whole = P()
    split = P("dp")
    placed = (split,) + (whole,) * 13 + (split, split)
    owned = P("dp", None, None, "pipe")
    return jax.shard_map(
        shards, mesh=mesh, in_specs=placed, out_specs=(owned, owned) + (whole,) * 13, check_vma=False
    )
```

time: 1810 us -> 93.3 us (0.05)
  waiting for transfers between devices: 866 us -> 0 us
  other arithmetic: 406 us -> 0 us
  local copies, waits for them, and re-layouts: 257 us -> 0 us
  loops' own time: 123 us -> 0 us
  Pallas kernels: 0 us -> 92.3 us
  blocking collectives: 70.1 us -> 0 us
  starting transfers between devices: 55.6 us -> 0 us
    ppermute x23 -> x0, waiting for transfers between devices: 700 us -> none  [from_behind(): return lax.ppermute(block, axis, route)]
    psum x1 -> x0, waiting for transfers between devices: 156 us -> none  [shards(): lax.psum((grads[0], grads[1], grads[2], grads[3], grads[4], grads[5], gra...]
    reduce_sum x36 -> x0, other arithmetic: 156 us -> none  [the longest x8 98.6 us: layer_norm(): mean = jnp.mean(values, axis=-1, keepdims=True)]
    another operation x14 -> x0, loops' own time: 123 us -> none  [the longest x7 113 us: shards(): lax.switch(branch_index, [backward_one, backward_two, backward_three, bac...]
    unnamed x138 -> x0, local copies, waits for them, and re-layouts: 106 us -> none
    mul x16 -> x0, other arithmetic: 105 us -> none  [depthwise(): padded[:, across:across + height, down:down + width, :]]
    pallas_call x0 -> x2, Pallas kernels: none -> 92.3 us  [the longest x1 85.7 us: whole_call(): pl.pallas_call(functools.partial(whole_kernel, own, ways, groups), out_sh...]
    add_any x4 -> x0, other arithmetic: 84.9 us -> none  [depthwise(): padded[:, across:across + height, down:down + width, :]]
  transfers between devices with their start and end apart: 26 -> 0, of which waited for: 19 -> 0; matrix products, arithmetic and copies ran while one was open for 12% -> 0% of each run, Pallas kernels for 0% -> 0%
where the time goes in v1:
time: 93.3 us; the launch traced here: 93.1 us
  Pallas kernels  92.3 us (99%)
    pallas_call x1, Pallas kernels, whole_call(): pl.pallas_call(functools.partial(whole_kernel, own, ways, groups), out_sh...  85.7 us
    pallas_call x1, Pallas kernels, finish_call(): pl.pallas_call(functools.partial(finish_kernel, own, ways), out_shape=sha...  6.61 us

profile of v1, /device:TPU:1, one launch (start us, length us, event | category | flops | bytes accessed | tf_op | source)
XLA Modules:
  0.0 93.1 jit_solution(5777410661953863638)
XLA Ops:
  0.7 85.7 %shard_map.325 = (bf16[4,1536,384]{2,1,0:T(8,128)(2,1)S(1)}, bf16[7,7,16,192]{3,2,1,0:T(8,128)(2,1)S(1)}, bf16[4,224,384]{2,1,0:T(8,128)(2,1)S(1)}, f32[64,384]{1,0:T(8,128)}) custom-call(s32[16]{0:T(128)} %refs_0_.1, f32[7,7,384]{2,1,0:T(8,128)} %refs_1_.1, f32[384]{0:T(512)} %refs_2_.1, f32[384]{0:T(512)} %refs_3_.1, f32[384]{0:T(512)} %refs_4_.1, ...), custom_call_target="tpu_custom_call" | custom-call | tf_op jit(solution)/shard_map/pallas_call | solution.py:874
  86.3 6.6 %shard_map.326 = (bf16[7,7,16,192]{3,2,1,0:T(8,128)(2,1)}, f32[14,14,16,96]{3,2,1,0:T(8,128)}, f32[7,7,384]{2,1,0:T(8,128)}, f32[384]{0:T(512)}, f32[384]{0:T(51...) custom-call(bf16[4,1536,384]{2,1,0:T(8,128)(2,1)S(1)} %get-tuple-ele, ...), custom_call_target="tpu_custom_call" | custom-call | tf_op jit(solution)/shard_map/pallas_call | solution.py:988

commit v2 on v1

--- a/solution.py
+++ b/solution.py
@@ -603,9 +603,7 @@
         self.came.append(copy)
 
     def add(self, target, start, slots, rows):
-        step = self.least
-        while step < 64 and rows % (2 * step) == 0:
-            step *= 2
+        step = max(size for size in range(self.least, min(rows, 192) + 1, self.least) if rows % size == 0)
 
         def one(t, carry):
             to = pl.ds(pl.multiple_of(start + t * step, self.least), step)
@@ -615,7 +613,10 @@
             target[to, :] = total
             return carry
 
-        lax.fori_loop(0, rows // step, one, 0)
+        if rows == step:
+            one(0, 0)
+        else:
+            lax.fori_loop(0, rows // step, one, 0)
 
     def reduce(self):
         start, rows, slots = self.start, self.rows, self.slots
@@ -654,7 +655,11 @@
         keep = 0
         if self.halving:
             keep = count * sum(bit * 2**k for k, (bit, _) in enumerate(bits))
-            self.path.append((axis, index, bits, start, rows))
+            at, size = start, rows
+            for bit in reversed(bits):
+                self.path.append((axis, index, [bit], at, size))
+                size //= 2
+                at = at + size * bit[0]
             if slots:
                 self.add(self.work, start + keep, [slot + keep for slot in slots], count)
         self.start, self.rows = start + keep, count
@@ -690,22 +695,25 @@
 PARTS = ((0, 0), (1, 0), (0, 768), (1, 768), (2, 0), (2, 768), (3, 0), (3, 768))
 IMAGE, MAPS = 100, 101
 SCHEDULE = {
-    "p0": (0,),
-    "p1": (3,),
-    "b": (0,),
-    "j0": (2, MAPS, 1),
-    "j": (3,),
-    "d1": (5, 4, 2, 1),
-    "s1": (0,),
-    "u0": (6, 5, 3, 0),
-    "u1": (4,),
-    "n": (2, 1, 7, 3, 0, 6),
-    "l2": (5, 7),
-    "l3": (3, 0, 1),
-    "l4": (2,),
-    "l5": (6, 5, 3),
-    "t": (8, 1, 4, 6),
-    "end": (7, 8, 2, 0, 1, 5, 4, 3, 6, 7, 2, 8, 5, IMAGE, 4, 1, 3, 0, 6, 7, 1, 8, 4, 2, 5, 7, 6, 2, 4, 8, 7, 4, 8, 6, 5, 7),
+    "p0": (1,),
+    "m": (0,),
+    "b": (1, 2),
+    "j": (MAPS, 0, 3),
+    "d0": (4,),
+    "d1": (2,),
+    "s3": (3, 1, 0, 5, 4),
+    "u0": (2, 6),
+    "u1": (1,),
+    "n0": (0, 5),
+    "l0": (7, 3),
+    "l1": (6, 2),
+    "l2": (4,),
+    "l3": (0, 3, 5, 7),
+    "l4": (1,),
+    "l5": (4, 2),
+    "i": (6,),
+    "t": (8, 5, 0, 1, 3, 7, 8, 6, 4, 5, 0, 2, 3, 7, 1, 6, 8, 4, 5, 7, 2, 3, IMAGE, 6, 7),
+    "end": (8, 1, 4, 5, 0, 2, 6, 7, 3, 1, 5, 4, 8, 0, 6, 7, 2, 5, 8, 3, 4, 6, 7),
 }
 
 
@@ -817,12 +825,13 @@
         pl.semaphore_signal(barrier, inc=1, device_id={axis: partner}, device_id_type=pl.DeviceIdType.MESH)
 
     steps = near + far
+    turned = [(axis, index, bits[::-1]) for axis, index, bits in steps], steps
 
     def part_sum(i, k, first):
         rows = pl.ds(first, 2 * C)
 
         return Sum(
-            s.grads.at[k, rows, :], s.land.at[i], total.at[k, rows, :], 2 * C, 16, steps,
+            s.grads.at[k, rows, :], s.land.at[i], total.at[k, rows, :], 2 * C, 16, turned[i % 2],
             (s.sum_send.at[i], s.sum_recv.at[i]),
         )
 

time: 93.3 us -> 91.4 us (0.980)
  Pallas kernels: 92.3 us -> 90.4 us
    pallas_call x1, Pallas kernels: 85.7 us -> 83.8 us  [whole_call(): pl.pallas_call(functools.partial(whole_kernel, own, ways, groups), out_sh...]
where the time goes in v2:
time: 91.4 us; the launch traced here: 91.2 us
  Pallas kernels  90.4 us (99%)
    pallas_call x1, Pallas kernels, whole_call(): pl.pallas_call(functools.partial(whole_kernel, own, ways, groups), out_sh...  83.8 us
    pallas_call x1, Pallas kernels, finish_call(): pl.pallas_call(functools.partial(finish_kernel, own, ways), out_shape=sha...  6.61 us

profile of v2, /device:TPU:1, one launch (start us, length us, event | category | flops | bytes accessed | tf_op | source)
XLA Modules:
  0.0 91.2 jit_solution(14701431206662932176)
XLA Ops:
  0.7 83.8 %shard_map.325 = (bf16[4,1536,384]{2,1,0:T(8,128)(2,1)S(1)}, bf16[7,7,16,192]{3,2,1,0:T(8,128)(2,1)S(1)}, bf16[4,224,384]{2,1,0:T(8,128)(2,1)S(1)}, f32[64,384]{1,0:T(8,128)}) custom-call(s32[16]{0:T(128)} %refs_0_.1, f32[7,7,384]{2,1,0:T(8,128)} %refs_1_.1, f32[384]{0:T(512)} %refs_2_.1, f32[384]{0:T(512)} %refs_3_.1, f32[384]{0:T(512)} %refs_4_.1, ...), custom_call_target="tpu_custom_call" | custom-call | tf_op jit(solution)/shard_map/pallas_call | solution.py:883
  84.5 6.6 %shard_map.326 = (bf16[7,7,16,192]{3,2,1,0:T(8,128)(2,1)}, f32[14,14,16,96]{3,2,1,0:T(8,128)}, f32[7,7,384]{2,1,0:T(8,128)}, f32[384]{0:T(512)}, f32[384]{0:T(51...) custom-call(bf16[4,1536,384]{2,1,0:T(8,128)(2,1)S(1)} %get-tuple-ele, ...), custom_call_target="tpu_custom_call" | custom-call | tf_op jit(solution)/shard_map/pallas_call | solution.py:997
